TPU v7x, 32 devices: a whole 2x2x4 slice. The times are simulated.
32 devices in a mesh: groups: 2 (over x), chan: 16 (over z, y, core).
Axes of the slice: x: 2, y: 2, z: 4, core: 2. Of those that a mesh axis runs over, the one named last changes fastest.
Arguments:
- raw: float32 [128, 2, 4352], P(('groups', 'chan')), parts along dimension 0, may hold values from -6 to 6
- fir: float32 [255], replicated, may hold values from -0.375 to 0.375
- spatial_taps: float32 [9], replicated, may hold values from -2 to 2
- flags: int32 [128, 2], P(('groups', 'chan')), parts along dimension 0, may hold values 0 or 1
- keep: int32 [64], replicated, may hold values 0 or 1
Outputs:
- correlations: bfloat16 [128, 101, 64], P(('groups', 'chan')), parts along dimension 0
There are 2 independent parts, one for each index of `groups`. A program takes and returns all parts, laid end to end along the dimension named above; an argument that names none is the same for every part. Nothing has to cross between parts.
All inputs are finite; a program needn't handle non-finite values. No bound on the sum of `flags` on one device may be relied on, other than what follows from the above.
Results may differ from a plain program's by a relative error of at most 0.0046.
Values may be sent and summed in bfloat16 or wider, within the bound.
A program may use at most 128 MiB of HBM per device.

v0:
```python
import math

import jax
import jax.numpy as jnp
from jax import lax
from jax.sharding import PartitionSpec as P

S = 2
W = 2
NT = 512
TAPS = 255
DEC = 4
SPAN = 9
LAGS = 101
NF = 256
TD = 1024
HALF = 4
HALFLAG = 50


def padded_2(cells, sides, width):
    for axis, dim in sides:
        count = lax.axis_size(axis)
        ends = count - 1
        head = lax.slice_in_dim(cells, 0, width, axis=dim)
        tail = lax.slice_in_dim(cells, cells.shape[dim] - width, cells.shape[dim], axis=dim)
        cells = jnp.concatenate(
            [
                lax.ppermute(tail, axis, [(i, (i + 1) % count) for i in range(ends)]),
                cells,
                lax.ppermute(head, axis, [((i + 1) % count, i) for i in range(ends)]),
            ],
            axis=dim,
        )
    return cells


def decimate(raw, fir):
    rows = raw.shape[0]
    segs = raw.shape[1]
    block = math.gcd(TD, 128)
    n_blocks = TD // block
    stride = DEC * block
    width = stride + TAPS + 1
    row_pos = (
        jnp.arange(width, dtype=jnp.int32)[:, None]
        - DEC * jnp.arange(block, dtype=jnp.int32)[None, :]
    )
    inside = (row_pos >= 0) & (row_pos < TAPS)
    toeplitz = jnp.where(inside, jnp.take(fir, jnp.clip(row_pos, 0, TAPS - 1)), 0.0)
    main_mat = toeplitz[:stride]
    tail_mat = toeplitz[stride:]
    extra = (n_blocks + 1) * stride - raw.shape[2]
    extended = jnp.concatenate([raw, jnp.zeros((rows, segs, extra), jnp.float32)], 2)
    blocks = extended.reshape(rows, segs, n_blocks + 1, stride)
    output = jnp.dot(
        blocks[:, :, :n_blocks],
        main_mat,
        precision=lax.Precision.HIGHEST,
        preferred_element_type=jnp.float32,
    )
    output = output + jnp.dot(
        blocks[:, :, 1:, : TAPS + 1],
        tail_mat,
        precision=lax.Precision.HIGHEST,
        preferred_element_type=jnp.float32,
    )
    return output.reshape(rows, segs, TD)


def spatial_filter(padded, spatial_taps, rows):
    filtered = spatial_taps[0] * padded[0:rows]
    for offset in range(1, SPAN):
        filtered = filtered + spatial_taps[offset] * padded[offset : offset + rows]
    return filtered


def tables():
    time_idx = jnp.arange(NT, dtype=jnp.int32)
    freq_idx = jnp.arange(NF, dtype=jnp.int32)
    phases = time_idx[:, None] * freq_idx[None, :] % NT
    angles = phases.astype(jnp.float32) * (2.0 * math.pi / NT)
    norm_factor = 1.0 / math.sqrt(NT)
    cosine = jnp.cos(angles) * norm_factor
    sine = -jnp.sin(angles) * norm_factor
    taper_win = 0.5 - 0.5 * jnp.cos(time_idx.astype(jnp.float32) * (2.0 * math.pi / NT))
    lag_idx = jnp.arange(LAGS, dtype=jnp.int32) - HALFLAG
    lag_phase = freq_idx[:, None] * lag_idx[None, :] % NT
    lag_angles = lag_phase.astype(jnp.float32) * (2.0 * math.pi / NT)
    one_sided = jnp.where(freq_idx == 0, 1.0, 2.0).astype(jnp.float32)[:, None] * (
        1.0 / (2.0 * math.sqrt(NF))
    )
    lag_table = jnp.concatenate(
        [one_sided * jnp.cos(lag_angles), -one_sided * jnp.sin(lag_angles)], 0
    )
    return (cosine, sine, taper_win, lag_table)


def whiten(filtered, flags, cosine, sine, taper_win):
    rows = filtered.shape[0]
    tapered = filtered.reshape(rows, S, W, NT) * taper_win
    real_part = jnp.dot(
        tapered, cosine, precision=lax.Precision.HIGHEST, preferred_element_type=jnp.float32
    )
    imag_part = jnp.dot(
        tapered, sine, precision=lax.Precision.HIGHEST, preferred_element_type=jnp.float32
    )
    amplitude = jnp.sqrt(real_part * real_part + imag_part * imag_part)
    factor = flags.astype(jnp.float32)[:, :, None, None] / jnp.maximum(amplitude, 0.25)
    whitened = jnp.stack(
        [(real_part * factor).astype(jnp.bfloat16), (imag_part * factor).astype(jnp.bfloat16)], 1
    )
    return whitened.reshape(rows, 2 * S * W, NF)


def on_device(raw, fir, spatial_taps, flags, keep):
    ch_dev = raw.shape[0]
    n_chan = lax.axis_size("chan")
    own_index = lax.axis_index("chan")
    total_ch = ch_dev * n_chan
    cosine, sine, taper_win, lag_table = tables()
    decimated = decimate(raw, fir)
    padded = padded_2(decimated, (("chan", 0),), HALF)
    filtered = spatial_filter(padded, spatial_taps, ch_dev)
    spectra = whiten(filtered, flags, cosine, sine, taper_win)
    flag_bf = flags.astype(jnp.bfloat16)
    first_row = own_index * ch_dev
    keep_sym = jnp.concatenate([jnp.flip(keep[1:]), keep])
    row_ids = first_row + jnp.arange(ch_dev, dtype=jnp.int32)

    def mask_row(row_id):
        return lax.dynamic_slice_in_dim(keep_sym, total_ch - 1 - row_id, total_ch)

    col_ids = jnp.arange(total_ch, dtype=jnp.int32)
    row_mask = (jax.vmap(mask_row)(row_ids) * (col_ids[None, :] != row_ids[:, None])).astype(
        jnp.float32
    )
    theirs = lax.all_gather(spectra, "chan", axis=0, tiled=True)
    half_rows = theirs.shape[1] // 2
    rotated = jnp.concatenate([-theirs[:, half_rows:], theirs[:, :half_rows]], 1)
    cross_re = jnp.einsum("iuf,juf->ijf", spectra, theirs, preferred_element_type=jnp.float32)
    cross_im = jnp.einsum("iuf,juf->ijf", spectra, rotated, preferred_element_type=jnp.float32)
    summed = jnp.einsum(
        "ijg,gl->ilj",
        jnp.concatenate([cross_re, cross_im], 2),
        lag_table,
        precision=lax.Precision.HIGHEST,
        preferred_element_type=jnp.float32,
    )
    counts = jnp.dot(
        flag_bf,
        lax.all_gather(flag_bf, "chan", axis=0, tiled=True).T,
        preferred_element_type=jnp.float32,
    )
    factor = row_mask / jnp.maximum(counts, 1.0)
    return (summed * factor[:, None, :]).astype(jnp.bfloat16)


def solution(mesh):
    placed = (P(("groups", "chan"), None, None), P(), P(), P(("groups", "chan"), None), P())
    return jax.shard_map(
        on_device,
        mesh=mesh,
        in_specs=placed,
        out_specs=P(("groups", "chan"), None, None),
        check_vma=False,
    )
```

profile of v0, /device:TPU:0, one launch (start us, length us, event | category | flops | bytes accessed | tf_op | source)
XLA Modules:
  0.0 693.0 jit_solution(14217001466481119728)
XLA Ops:
  0.0 0.0 copy-start
  0.0 0.2 fusion.23
  0.2 0.5 copy-done
  0.7 611.7 %gather_fusion = f32[98304]{0:T(1024)S(1)} fusion(f32[255]{0:T(256)S(1)} %copy-done, s32[98304]{0:T(1024)S(1)} %fusion.23), kind=kCustom, calls=%fused_computation | custom fusion | bytes 1179648 | tf_op jit(solution)/shard_map/jit(_take)/gather | solution.py:50
  612.4 0.2 fusion.24
  612.6 0.0 copy-done.1
  612.6 0.1 concatenate.27
  612.7 0.1 reshape.120
  612.8 0.3 fusion.31
  613.1 0.2 convolution_add_fusion
  613.4 2.4 collective-permute-start
  615.7 1.3 collective-permute-start.1
  617.1 0.0 copy-done.2
  617.1 0.7 fusion.74
  617.8 0.0 copy-done.3
  617.8 24.9 %all-gather = bf16[16,4,2]{1,2,0:T(2,128)(2,1)S(1)} all-gather(bf16[1,4,2]{1,2,0:T(2,128)(2,1)S(1)} %get-tuple-element.27), channel_id=1, replica_groups=mesh['groups'=2,'chan'=16] {'chan'}, dimensions={0}, use_global_device_ids=true | all-gather | bytes 272 | tf_op jit(solution)/shard_map/all_gather | solution.py:152
  642.7 0.1 reshape.148
  642.8 0.1 slice.93
  642.9 0.1 rev.4
  643.0 0.1 pad_add_fusion
  643.1 5.4 while.2
  643.1 0.6 constant_dynamic-slice_fusion.3
  643.7 0.7 dynamic-slice_bitcast_fusion.3
  644.4 0.6 constant_dynamic-slice_fusion.3
  645.0 0.7 dynamic-slice_bitcast_fusion.3
  645.8 0.6 constant_dynamic-slice_fusion.3
  646.4 0.7 dynamic-slice_bitcast_fusion.3
  647.1 0.6 constant_dynamic-slice_fusion.3
  647.7 0.7 dynamic-slice_bitcast_fusion.3
  648.5 0.5 cosine_multiply_fusion
  649.0 0.2 fusion.2
  649.2 0.1 multiply_subtract_fusion
  649.2 0.0 collective-permute-done
  649.3 0.0 collective-permute-done.1
  649.3 5.7 fusion.47
  655.1 2.3 fusion.10
  657.4 2.3 fusion.56
  659.8 0.2 copy.23
  660.0 18.3 %all_gather.6 = bf16[64,8,256]{2,1,0:T(8,128)(2,1)S(1)} all-gather(bf16[4,8,256]{2,1,0:T(8,128)(2,1)S(1)} %copy.21), channel_id=1, replica_groups=mesh['groups'=2,'chan'=16] {'chan'}, dimensions={0}, use_global_device_ids=true | all-gather | bytes 278528 | tf_op jit(solution)/shard_map/all_gather | solution.py:138
  678.3 6.4 copy.22
  684.7 0.1 fusion.73
  684.8 0.2 copy.33
  685.0 0.1 neg.16
  685.1 0.2 copy.34
  685.3 4.4 convolution_bitcast_fusion.1
  689.8 0.5 convolution_bitcast_fusion
  690.3 0.3 pad_maximum_fusion
  690.6 2.4 fusion.1
  (24 shorter events, 0.3 us)
Async XLA Ops:
  0.0 0.7 copy-start
  0.7 612.0 %copy-start.1 = (f32[4,2,4352]{2,1,0:T(2,128)S(1)}, f32[4,2,4352]{2,1,0:T(2,128)}, u32[]{:S(2)}) copy-start(f32[4,2,4352]{2,1,0:T(2,128)} %param.5) | copy-start | bytes 417796
  0.7 616.4 %copy-start.2 = (f32[9]{0:T(128)S(1)}, f32[9]{0:T(128)}, u32[]{:S(2)}) copy-start(f32[9]{0:T(128)} %param.7) | copy-start | bytes 112
  0.7 617.1 %copy-start.3 = (s32[4,2]{0,1:T(2,128)S(1)}, s32[4,2]{0,1:T(2,128)}, u32[]{:S(2)}) copy-start(s32[4,2]{0,1:T(2,128)} %param.8) | copy-start | bytes 100
  0.7 642.1 %copy-start.4 = (s32[64]{0:T(128)S(1)}, s32[64]{0:T(128)}, u32[]{:S(2)}) copy-start(s32[64]{0:T(128)} %param.9) | copy-start | bytes 772
  613.4 35.9 %collective-permute-start = (f32[4,2,1024]{2,1,0:T(2,128)S(1)}, f32[4,2,1024]{2,1,0:T(2,128)S(1)}, u32[]{:S(2)}, u32[]{:S(2)}) collective-permute-start(f32[4,2,1024]{2,1,0:T(2,128)S(1)} %reshape.121), channel_id=1, source_target_pairs={{0,1},{1,2},{2,3},{3,4},{4,5},{5,6},{6,7},{7,8},{8,9},{9,10},{10,1... | collective-permute-start | bytes 98312 | tf_op jit(solution)/shard_map/ppermute | solution.py:29
  615.7 33.6 %collective-permute-start.1 = (f32[4,2,1024]{2,1,0:T(2,128)S(1)}, f32[4,2,1024]{2,1,0:T(2,128)S(1)}, u32[]{:S(2)}, u32[]{:S(2)}) collective-permute-start(f32[4,2,1024]{2,1,0:T(2,128)S(1)} %reshape.121), channel_id=1, source_target_pairs={{1,0},{2,1},{3,2},{4,3},{5,4},{6,5},{7,6},{8,7},{9,8},{10,9},{11,1... | collective-permute-start | bytes 98312 | tf_op jit(solution)/shard_map/ppermute | solution.py:31
where the time goes:
time: 693 us
  local copies, waits for them, and re-layouts  626 us (90%)
  blocking collectives  43.2 us (6%)
  matrix products  12.7 us (2%)
  other arithmetic  7.18 us (1%)
    gather x1, local copies, waits for them, and re-layouts, decimate(): jnp.take(fir, jnp.clip(row_pos, 0, TAPS - 1))  612 us
    all_gather x1, blocking collectives, on_device(): lax.all_gather(flag_bf, 'chan', axis=0, tiled=True)  24.9 us
    all_gather x1, blocking collectives, on_device(): theirs = lax.all_gather(spectra, 'chan', axis=0, tiled=True)  18.3 us
  transfers between devices with their start and end apart: 2, of which 0 were waited for; matrix products, arithmetic and copies ran while one was open for 1% of the time, Pallas kernels for 0%

commit v1 on v0

v1 whole, which is shorter than its diff:
```python
import functools
import math

import jax
import jax.numpy as jnp
import ml_dtypes
import numpy as np
from jax import lax
from jax.experimental import pallas as pl
from jax.experimental.pallas import tpu as pltpu
from jax.sharding import PartitionSpec as P

S = 2
W = 2
NT = 512
TAPS = 255
DEC = 4
SPAN = 9
LAGS = 101
NF = 256
TD = 1024
HALFLAG = 50
ROWS = 32
LAG_ROWS = 112
BLOCK = 128
REACH = DEC * BLOCK + TAPS + 1
COLS = 16
MESH = pl.DeviceIdType.MESH


def halves(values):
    high = values.astype(ml_dtypes.bfloat16)
    return high, (values - high.astype(np.float64)).astype(ml_dtypes.bfloat16)


def dft_table():
    time = np.arange(NT)
    angles = (time[:, None] * np.arange(NF)[None, :] % NT) * (2.0 * math.pi / NT)
    taper = (0.5 - 0.5 * np.cos(time * (2.0 * math.pi / NT))) / math.sqrt(NT)
    sine = -np.sin(angles)
    sine[:, 0] = 0.0
    table = np.concatenate([np.cos(angles), sine], 1) * taper[:, None]
    return np.concatenate(halves(table), 1)


def lag_table():
    freq = np.arange(NF)
    lags = np.arange(LAGS) - HALFLAG
    angles = (lags[:, None] * freq[None, :] % NT) * (2.0 * math.pi / NT)
    one_sided = np.where(freq == 0, 1.0, 2.0) / (2.0 * math.sqrt(NF))
    table = np.zeros((LAG_ROWS, 2 * NF))
    table[:LAGS, :NF] = one_sided * np.cos(angles)
    table[:LAGS, NF:] = -one_sided * np.sin(angles)
    table[:LAGS, NF] = 0.0
    table[LAGS, NF] = 0.5
    return np.concatenate(halves(table), 0)


def split(values):
    high = values.astype(jnp.bfloat16)
    return high, (values - high.astype(jnp.float32)).astype(jnp.bfloat16)


def product_nt(left, right):
    return lax.dot_general(
        left, right, (((1,), (1,)), ((), ())), preferred_element_type=jnp.float32
    )


def kernel(
    n,
    raw_ref,
    fir_ref,
    taps_ref,
    flags_ref,
    keep_ref,
    dft_hbm,
    lag_hbm,
    out_ref,
    dft_ref,
    lag_ref,
    firs_ref,
    pad_ref,
    filt_ref,
    dup_ref,
    spec_ref,
    turn_ref,
    own_ref,
    own_turn_ref,
    all_ref,
    cross_hi_ref,
    cross_lo_ref,
    table_sem,
    halo_send,
    halo_recv,
    send_sem,
    recv_sem,
):
    me = lax.axis_index("chan")
    total_ch = 4 * n

    dft_copy = pltpu.make_async_copy(dft_hbm, dft_ref, table_sem.at[0])
    lag_copy = pltpu.make_async_copy(lag_hbm, lag_ref, table_sem.at[1])
    dft_copy.start()
    lag_copy.start()

    barrier = pltpu.get_barrier_semaphore()

    def greet(k, carry):
        peer = lax.rem(me + k, n)
        pl.semaphore_signal(barrier, inc=1, device_id={"chan": peer}, device_id_type=MESH)
        return carry

    lax.fori_loop(1, n, greet, 0)

    firs_ref[...] = jnp.zeros_like(firs_ref)
    firs_ref[:, 0:TAPS] = jnp.broadcast_to(fir_ref[...], (32, TAPS))
    shifted = firs_ref[...]
    row_id = lax.broadcasted_iota(jnp.int32, shifted.shape, 0)
    for bit in range(5):
        moved = pltpu.roll(shifted, DEC << bit, 1)
        shifted = jnp.where((row_id // (1 << bit)) % 2 == 1, moved, shifted)
    pieces = []
    for part in range(4):
        row = []
        if part:
            row.append(jnp.zeros((32, 128 * part), jnp.float32))
        row.append(shifted)
        if part < 3:
            row.append(jnp.zeros((32, REACH - 384 - 128 * part), jnp.float32))
        pieces.append(jnp.concatenate(row, 1))
    filter_hi, filter_lo = split(jnp.concatenate(pieces, 0))
    raw = jnp.concatenate([raw_ref[c] for c in range(4)], 0)
    blocks = jnp.concatenate(
        [raw[:, DEC * BLOCK * b : DEC * BLOCK * b + REACH] for b in range(TD // BLOCK)], 0
    )
    raw_hi, raw_lo = split(blocks)
    sums = product_nt(
        jnp.concatenate([raw_hi, raw_lo], 0), jnp.concatenate([filter_hi, filter_lo], 0)
    )
    count = 8 * (TD // BLOCK)
    sums = sums[:count, :BLOCK] + (
        sums[count:, :BLOCK] + sums[:count, BLOCK:] + sums[count:, BLOCK:]
    )
    for b in range(TD // BLOCK):
        pad_ref[8:16, BLOCK * b : BLOCK * (b + 1)] = sums[8 * b : 8 * b + 8]

    pl.semaphore_wait(barrier, n - 1)

    to_right = pltpu.make_async_remote_copy(
        src_ref=pad_ref.at[8:16],
        dst_ref=pad_ref.at[0:8],
        send_sem=halo_send.at[0],
        recv_sem=halo_recv.at[0],
        device_id={"chan": lax.rem(me + 1, n)},
        device_id_type=MESH,
    )
    to_left = pltpu.make_async_remote_copy(
        src_ref=pad_ref.at[8:16],
        dst_ref=pad_ref.at[16:24],
        send_sem=halo_send.at[1],
        recv_sem=halo_recv.at[1],
        device_id={"chan": lax.rem(me + n - 1, n)},
        device_id_type=MESH,
    )

    @pl.when(me < n - 1)
    def _():
        to_right.start()

    @pl.when(me > 0)
    def _():
        to_left.start()

    masks = []
    keep = jnp.broadcast_to(keep_ref[...].astype(jnp.float32), (16, total_ch))
    keep = keep.astype(jnp.bfloat16)
    for chunk in range(n // COLS):
        lane = lax.broadcasted_iota(jnp.int32, (total_ch, 4 * 4 * COLS), 1)
        dist = lax.broadcasted_iota(jnp.int32, (total_ch, 4 * 4 * COLS), 0)
        gap = jnp.abs(
            4 * me + lane // (4 * COLS) - (lane % (4 * COLS) + chunk * 4 * COLS)
        )
        hit = jnp.where((gap == dist) & (dist > 0), 1.0, 0.0).astype(jnp.bfloat16)
        masks.append(jnp.dot(keep, hit, preferred_element_type=jnp.float32)[0:1])

    @pl.when(me > 0)
    def _():
        to_right.wait_recv()

    @pl.when(me == 0)
    def _():
        pad_ref[0:8] = jnp.zeros((8, TD), jnp.float32)

    @pl.when(me < n - 1)
    def _():
        to_left.wait_recv()

    @pl.when(me == n - 1)
    def _():
        pad_ref[16:24] = jnp.zeros((8, TD), jnp.float32)

    filtered = taps_ref[0] * pad_ref[0:8]
    for offset in range(1, SPAN):
        filtered = filtered + taps_ref[offset] * pad_ref[2 * offset : 2 * offset + 8]
    for tile in range(TD // 128):
        filt_ref[8 * tile : 8 * tile + 8] = filtered[:, 128 * tile : 128 * (tile + 1)]
    for s in range(S):
        for tile in range(TD // 128):
            one = filt_ref[pl.ds(8 * tile + s, 4, stride=2), :]
            dup_ref[8 * s : 8 * s + 4, 128 * tile : 128 * (tile + 1)] = one
            dup_ref[8 * s + 4 : 8 * s + 8, 128 * tile : 128 * (tile + 1)] = one
    windows = jnp.concatenate(
        [dup_ref[8 * s : 8 * s + 8, NT * w : NT * (w + 1)] for s in range(S) for w in range(W)], 0
    )
    win_hi, win_lo = split(windows)
    dft_copy.wait()
    spectra = jnp.dot(
        jnp.concatenate([win_hi, win_lo], 0), dft_ref[...], preferred_element_type=jnp.float32
    )
    spectra = spectra[:ROWS, : 2 * NF] + (
        spectra[ROWS:, : 2 * NF] + spectra[:ROWS, 2 * NF :] + spectra[ROWS:, 2 * NF :]
    )
    real, imag = spectra[:, :NF], spectra[:, NF:]
    rows = lax.broadcasted_iota(jnp.int32, (ROWS, NF), 0)
    lanes = lax.broadcasted_iota(jnp.int32, (ROWS, NF), 1)
    flag = jnp.zeros((ROWS, NF), jnp.float32)
    for s in range(S):
        for c in range(4):
            here = (rows // 16 == s) & (rows % 4 == c)
            flag = jnp.where(here, flags_ref[c, s].astype(jnp.float32), flag)
    factor = flag / jnp.maximum(jnp.sqrt(real * real + imag * imag), 0.25)
    is_real = (rows // 4) % 2 == 0
    real = (real * factor).astype(jnp.bfloat16).astype(jnp.float32)
    imag = (imag * factor).astype(jnp.bfloat16).astype(jnp.float32)
    stash = (lanes == 0) & (~is_real)
    spec = jnp.where(is_real, real, imag)
    all_ref[me] = jnp.where(stash, flag, spec).astype(jnp.bfloat16)

    def copy_to(k):
        return pltpu.make_async_remote_copy(
            src_ref=all_ref.at[me],
            dst_ref=all_ref.at[me],
            send_sem=send_sem.at[k],
            recv_sem=recv_sem.at[me],
            device_id={"chan": lax.rem(me + k, n)},
            device_id_type=MESH,
        )

    def send(k, carry):
        copy_to(k).start()
        return carry

    lax.fori_loop(1, n, send, 0)

    spec_ref[...] = jnp.where(stash, 0.0, spec)
    turn_ref[...] = jnp.where(stash, flag, jnp.where(is_real, imag, -real))
    upper = lax.broadcasted_iota(jnp.int32, (8, NF), 0) < 4
    for ref, target in ((spec_ref, own_ref), (turn_ref, own_turn_ref)):
        for i in range(4):
            for k in range(S * W):
                first = jnp.broadcast_to(ref[8 * k + i : 8 * k + i + 1], (8, NF))
                second = jnp.broadcast_to(ref[8 * k + 4 + i : 8 * k + 5 + i], (8, NF))
                target[i, 8 * k : 8 * k + 8] = jnp.where(upper, first, second)
    lag_copy.wait()

    def receive(k, carry):
        src = lax.rem(me + k, n)
        pltpu.make_async_remote_copy(
            src_ref=all_ref.at[src],
            dst_ref=all_ref.at[src],
            send_sem=send_sem.at[k],
            recv_sem=recv_sem.at[src],
            device_id={"chan": src},
            device_id_type=MESH,
        ).wait_recv()
        return carry

    lax.fori_loop(1, n, receive, 0)

    for chunk in range(n // COLS):

        def quad(q, carry):
            base = chunk * COLS + 4 * q
            for i in range(4):
                for half, ref in enumerate((own_ref, own_turn_ref)):
                    sums = []
                    for d in range(4):
                        theirs = all_ref[base + d].astype(jnp.float32)
                        acc = ref[i, 0:8] * theirs[0:8]
                        for k in range(1, S * W):
                            acc = acc + ref[i, 8 * k : 8 * k + 8] * theirs[8 * k : 8 * k + 8]
                        sums.append(acc)
                    both = []
                    for d in (0, 2):
                        a, b = sums[d], sums[d + 1]
                        both.append(
                            jnp.where(upper, a, b) + pltpu.roll(jnp.where(upper, b, a), 4, 0)
                        )
                    high, low = split(jnp.concatenate(both, 0))
                    at = pl.ds(pl.multiple_of(4 * COLS * i + 16 * q, 16), 16)
                    cross_hi_ref[at, NF * half : NF * (half + 1)] = high
                    cross_lo_ref[at, NF * half : NF * (half + 1)] = low
            return carry

        lax.fori_loop(0, COLS // 4, quad, 0)
        lag = lag_ref[...]
        summed = product_nt(lag, cross_hi_ref[...])
        summed = (
            summed[:LAG_ROWS]
            + summed[LAG_ROWS:]
            + product_nt(lag[:LAG_ROWS], cross_lo_ref[...])
        )
        scale = masks[chunk] / jnp.maximum(summed[LAGS : LAGS + 1], 1.0)
        result = (summed * scale).astype(jnp.bfloat16)
        for i in range(4):
            out_ref[i, :, 4 * COLS * chunk : 4 * COLS * (chunk + 1)] = result[
                :LAGS, 4 * COLS * i : 4 * COLS * (i + 1)
            ]

    def sent(k, carry):
        copy_to(k).wait_send()
        return carry

    lax.fori_loop(1, n, sent, 0)

    @pl.when(me < n - 1)
    def _():
        to_right.wait_send()

    @pl.when(me > 0)
    def _():
        to_left.wait_send()


def on_device(raw, fir, spatial_taps, flags, keep):
    n = lax.axis_size("chan")
    vmem = pl.BlockSpec(memory_space=pltpu.VMEM)
    smem = pl.BlockSpec(memory_space=pltpu.SMEM)
    anywhere = pl.BlockSpec(memory_space=pl.ANY)
    return pl.pallas_call(
        functools.partial(kernel, n),
        out_shape=jax.ShapeDtypeStruct((4, LAGS, 4 * n), jnp.bfloat16),
        in_specs=[vmem, vmem, smem, smem, vmem, anywhere, anywhere],
        out_specs=vmem,
        scratch_shapes=[
            pltpu.VMEM((NT, 4 * NF), jnp.bfloat16),
            pltpu.VMEM((2 * LAG_ROWS, 2 * NF), jnp.bfloat16),
            pltpu.VMEM((32, 384), jnp.float32),
            pltpu.VMEM((24, TD), jnp.float32),
            pltpu.VMEM((TD // 16, 128), jnp.float32),
            pltpu.VMEM((16, TD), jnp.float32),
            pltpu.VMEM((ROWS, NF), jnp.float32),
            pltpu.VMEM((ROWS, NF), jnp.float32),
            pltpu.VMEM((4, ROWS, NF), jnp.float32),
            pltpu.VMEM((4, ROWS, NF), jnp.float32),
            pltpu.VMEM((n, ROWS, NF), jnp.bfloat16),
            pltpu.VMEM((16 * COLS, 2 * NF), jnp.bfloat16),
            pltpu.VMEM((16 * COLS, 2 * NF), jnp.bfloat16),
            pltpu.SemaphoreType.DMA((2,)),
            pltpu.SemaphoreType.DMA((2,)),
            pltpu.SemaphoreType.DMA((2,)),
            pltpu.SemaphoreType.DMA((n,)),
            pltpu.SemaphoreType.DMA((n,)),
        ],
        compiler_params=pltpu.CompilerParams(
            collective_id=0, has_side_effects=True, vmem_limit_bytes=32 * 2**20
        ),
    )(
        raw,
        fir.reshape(1, TAPS),
        spatial_taps,
        flags,
        keep.reshape(1, 4 * n),
        jnp.asarray(dft_table()),
        jnp.asarray(lag_table()),
    )


def solution(mesh):
    placed = (P(("groups", "chan"), None, None), P(), P(), P(("groups", "chan"), None), P())
    return jax.shard_map(
        on_device,
        mesh=mesh,
        in_specs=placed,
        out_specs=P(("groups", "chan"), None, None),
        check_vma=False,
    )
```

time: 693 us -> 21.9 us (0.03)
  local copies, waits for them, and re-layouts: 626 us -> 5.17 us
  blocking collectives: 43.2 us -> 0 us
  Pallas kernels: 0 us -> 16.5 us
  matrix products: 12.7 us -> 0 us
  other arithmetic: 7.18 us -> 0 us
    gather x13 -> x0, local copies, waits for them, and re-layouts: 617 us -> none  [the longest x1 612 us: decimate(): jnp.take(fir, jnp.clip(row_pos, 0, TAPS - 1))]
    all_gather x2 -> x0, blocking collectives: 43.2 us -> none  [the longest x1 24.9 us: on_device(): lax.all_gather(flag_bf, 'chan', axis=0, tiled=True)]
    pallas_call x0 -> x1, Pallas kernels: none -> 16.5 us  [on_device(): pl.pallas_call(functools.partial(kernel, n), out_shape=jax.ShapeDtypeStru...]
    dot_general x8 -> x0, matrix products: 12.7 us -> none  [the longest x1 4.44 us: on_device(): jnp.einsum('iuf,juf->ijf', spectra, theirs, preferred_element_type=jnp.fl...]
  transfers between devices with their start and end apart: 2 -> 0, of which waited for: 0 -> 0; matrix products, arithmetic and copies ran while one was open for 1% -> 0% of each run, Pallas kernels for 0% -> 0%
where the time goes in v1:
time: 21.9 us; the launch traced here: 21.7 us
  Pallas kernels  16.5 us (75%)
  local copies, waits for them, and re-layouts  5.17 us (24%)
    pallas_call x1, Pallas kernels, on_device(): pl.pallas_call(functools.partial(kernel, n), out_shape=jax.ShapeDtypeStru...  16.5 us
    unnamed x15, local copies, waits for them, and re-layouts  4.43 us
    pallas_call x1, local copies, waits for them, and re-layouts, on_device(): pl.pallas_call(functools.partial(kernel, n), out_shape=jax.ShapeDtypeStru...  0.73 us

profile of v1, /device:TPU:0, one launch (start us, length us, event | category | flops | bytes accessed | tf_op | source)
XLA Modules:
  0.0 21.7 jit_solution(12640817739757004653)
XLA Ops:
  0.0 0.0 copy-start.6
  0.0 0.7 %copy-done.6 = s32[4,2]{0,1:T(2,128)S(1)} copy-done((s32[4,2]{0,1:T(2,128)S(1)}, s32[4,2]{0,1:T(2,128)}, u32[]{:S(2)}) %copy-start.6) | copy-done | bytes 56
  0.7 0.0 copy-start.3
  0.7 0.0 copy-start.4
  0.7 0.0 copy-start.5
  0.7 0.1 copy.8.flags_ref
  0.8 0.6 %copy-done.3 = f32[255]{0:T(256)S(1)} copy-done((f32[255]{0:T(256)S(1)}, f32[255]{0:T(256)}, u32[]{:S(2)}) %copy-start.3) | copy-done | bytes 1044
  1.4 0.0 copy-done.4
  1.4 0.0 copy-done.5
  1.4 0.0 copy-start
  1.4 1.2 %copy-done = bf16[512,1024]{1,0:T(8,128)(2,1)S(1)} copy-done((bf16[512,1024]{1,0:T(8,128)(2,1)S(1)}, bf16[512,1024]{1,0:T(8,128)(2,1)}, u32[]{:S(2)}) %copy-start) | copy-done | bytes 1048600
  2.6 0.0 copy-start.1
  2.6 0.9 %copy-done.1 = bf16[224,512]{1,0:T(8,128)(2,1)S(1)} copy-done((bf16[224,512]{1,0:T(8,128)(2,1)S(1)}, bf16[224,512]{1,0:T(8,128)(2,1)}, u32[]{:S(2)}) %copy-start.1) | copy-done | bytes 229400
  3.5 0.0 copy-start.2
  3.5 0.9 %copy-done.2 = f32[4,2,4352]{2,1,0:T(2,128)S(1)} copy-done((f32[4,2,4352]{2,1,0:T(2,128)S(1)}, f32[4,2,4352]{2,1,0:T(2,128)}, u32[]{:S(2)}) %copy-start.2) | copy-done | bytes 139288
  4.4 16.5 %shard_map.73 = bf16[4,101,64]{2,1,0:T(8,128)(2,1)S(1)} custom-call(f32[4,2,4352]{2,1,0:T(2,128)S(1)} %copy-done.2, f32[1,255]{1,0:T(1,128)S(1)} %bitcast.2, f32[9]{0:T(128)S(1)} %copy-done.4, s32[4,2]{1,0:T(4,128)S(1)} %copy.8.flags_ref, s32[1,64]{1,0:T(1,128)S(1)} %bitcast.3, bf16[512,1024]{1,0:T(8,128)(2,1)S(1)} %copy-done, bf16[224,512]{1,0:T(8,128)(2,1)S(1)} %copy-done.1), custom_call_target="tpu_custom_call" | custom-call | tf_op jit(solution)/shard_map/pallas_call | solution.py:341
  20.9 0.7 %copy.9 = bf16[4,101,64]{1,2,0:T(8,128)(2,1)} copy(bf16[4,101,64]{2,1,0:T(8,128)(2,1)S(1)} %shard_map.73) | data formatting | bytes 103424 | tf_op jit(solution)/shard_map/pallas_call | solution.py:341
Async XLA Ops:
  0.0 0.7 %copy-start.6 = (s32[4,2]{0,1:T(2,128)S(1)}, s32[4,2]{0,1:T(2,128)}, u32[]{:S(2)}) copy-start(s32[4,2]{0,1:T(2,128)} %param.10) | copy-start | bytes 100
  0.7 0.7 %copy-start.3 = (f32[255]{0:T(256)S(1)}, f32[255]{0:T(256)}, u32[]{:S(2)}) copy-start(f32[255]{0:T(256)} %param.8) | copy-start | bytes 3064
  0.7 0.7 %copy-start.4 = (f32[9]{0:T(128)S(1)}, f32[9]{0:T(128)}, u32[]{:S(2)}) copy-start(f32[9]{0:T(128)} %taps_ref.1) | copy-start | bytes 112
  0.7 0.7 %copy-start.5 = (s32[64]{0:T(128)S(1)}, s32[64]{0:T(128)}, u32[]{:S(2)}) copy-start(s32[64]{0:T(128)} %param.11) | copy-start | bytes 772
  1.4 1.2 %copy-start = (bf16[512,1024]{1,0:T(8,128)(2,1)S(1)}, bf16[512,1024]{1,0:T(8,128)(2,1)}, u32[]{:S(2)}) copy-start(bf16[512,1024]{1,0:T(8,128)(2,1)} %constant.4.clone.dft_hbm) | copy-start | bytes 3145732
  2.6 0.9 %copy-start.1 = (bf16[224,512]{1,0:T(8,128)(2,1)S(1)}, bf16[224,512]{1,0:T(8,128)(2,1)}, u32[]{:S(2)}) copy-start(bf16[224,512]{1,0:T(8,128)(2,1)} %constant.5.clone.lag_hbm) | copy-start | bytes 688132
  3.5 0.9 %copy-start.2 = (f32[4,2,4352]{2,1,0:T(2,128)S(1)}, f32[4,2,4352]{2,1,0:T(2,128)}, u32[]{:S(2)}) copy-start(f32[4,2,4352]{2,1,0:T(2,128)} %raw_ref.1) | copy-start | bytes 417796

commit v2 on v1

--- a/solution.py
+++ b/solution.py
@@ -21,7 +21,7 @@
 TD = 1024
 HALFLAG = 50
 ROWS = 32
-LAG_ROWS = 112
+LAG_ROWS = 128
 BLOCK = 128
 REACH = DEC * BLOCK + TAPS + 1
 COLS = 16
@@ -69,14 +69,19 @@
 
 def kernel(
     n,
+    raw_hbm,
+    fir_hbm,
+    taps_hbm,
+    flags_hbm,
+    keep_hbm,
+    dft_hbm,
+    lag_hbm,
+    out_ref,
     raw_ref,
     fir_ref,
     taps_ref,
     flags_ref,
     keep_ref,
-    dft_hbm,
-    lag_hbm,
-    out_ref,
     dft_ref,
     lag_ref,
     firs_ref,
@@ -99,10 +104,21 @@
     me = lax.axis_index("chan")
     total_ch = 4 * n
 
-    dft_copy = pltpu.make_async_copy(dft_hbm, dft_ref, table_sem.at[0])
-    lag_copy = pltpu.make_async_copy(lag_hbm, lag_ref, table_sem.at[1])
-    dft_copy.start()
-    lag_copy.start()
+    pairs = (
+        (fir_hbm, fir_ref),
+        (raw_hbm, raw_ref),
+        (dft_hbm, dft_ref),
+        (taps_hbm, taps_ref),
+        (flags_hbm, flags_ref),
+        (keep_hbm, keep_ref),
+        (lag_hbm, lag_ref),
+    )
+    copies = [
+        pltpu.make_async_copy(src, dst, table_sem.at[k]) for k, (src, dst) in enumerate(pairs)
+    ]
+    for copy in copies:
+        copy.start()
+    fir_copy, raw_copy, dft_copy, taps_copy, flags_copy, keep_copy, lag_copy = copies
 
     barrier = pltpu.get_barrier_semaphore()
 
@@ -114,6 +130,7 @@
     lax.fori_loop(1, n, greet, 0)
 
     firs_ref[...] = jnp.zeros_like(firs_ref)
+    fir_copy.wait()
     firs_ref[:, 0:TAPS] = jnp.broadcast_to(fir_ref[...], (32, TAPS))
     shifted = firs_ref[...]
     row_id = lax.broadcasted_iota(jnp.int32, shifted.shape, 0)
@@ -130,6 +147,7 @@
             row.append(jnp.zeros((32, REACH - 384 - 128 * part), jnp.float32))
         pieces.append(jnp.concatenate(row, 1))
     filter_hi, filter_lo = split(jnp.concatenate(pieces, 0))
+    raw_copy.wait()
     raw = jnp.concatenate([raw_ref[c] for c in range(4)], 0)
     blocks = jnp.concatenate(
         [raw[:, DEC * BLOCK * b : DEC * BLOCK * b + REACH] for b in range(TD // BLOCK)], 0
@@ -173,16 +191,16 @@
         to_left.start()
 
     masks = []
-    keep = jnp.broadcast_to(keep_ref[...].astype(jnp.float32), (16, total_ch))
-    keep = keep.astype(jnp.bfloat16)
+    keep_copy.wait()
+    keep = jnp.broadcast_to(keep_ref[...].astype(jnp.float32), (16 * COLS, total_ch))
+    row = lax.broadcasted_iota(jnp.int32, keep.shape, 0)
+    dist = lax.broadcasted_iota(jnp.int32, keep.shape, 1)
     for chunk in range(n // COLS):
-        lane = lax.broadcasted_iota(jnp.int32, (total_ch, 4 * 4 * COLS), 1)
-        dist = lax.broadcasted_iota(jnp.int32, (total_ch, 4 * 4 * COLS), 0)
-        gap = jnp.abs(
-            4 * me + lane // (4 * COLS) - (lane % (4 * COLS) + chunk * 4 * COLS)
-        )
-        hit = jnp.where((gap == dist) & (dist > 0), 1.0, 0.0).astype(jnp.bfloat16)
-        masks.append(jnp.dot(keep, hit, preferred_element_type=jnp.float32)[0:1])
+        gap = jnp.abs(4 * me + row // (4 * COLS) - (row % (4 * COLS) + chunk * 4 * COLS))
+        hit = jnp.where((gap == dist) & (dist > 0), keep, 0.0)
+        masks.append(jnp.sum(hit, axis=1, keepdims=True))
+    taps_copy.wait()
+    flags_copy.wait()
 
     @pl.when(me > 0)
     def _():
@@ -228,7 +246,7 @@
     for s in range(S):
         for c in range(4):
             here = (rows // 16 == s) & (rows % 4 == c)
-            flag = jnp.where(here, flags_ref[c, s].astype(jnp.float32), flag)
+            flag = jnp.where(here, flags_ref[s, c].astype(jnp.float32), flag)
     factor = flag / jnp.maximum(jnp.sqrt(real * real + imag * imag), 0.25)
     is_real = (rows // 4) % 2 == 0
     real = (real * factor).astype(jnp.bfloat16).astype(jnp.float32)
@@ -305,17 +323,17 @@
 
         lax.fori_loop(0, COLS // 4, quad, 0)
         lag = lag_ref[...]
-        summed = product_nt(lag, cross_hi_ref[...])
+        summed = product_nt(cross_hi_ref[...], lag)
         summed = (
-            summed[:LAG_ROWS]
-            + summed[LAG_ROWS:]
-            + product_nt(lag[:LAG_ROWS], cross_lo_ref[...])
+            summed[:, :LAG_ROWS]
+            + summed[:, LAG_ROWS:]
+            + product_nt(cross_lo_ref[...], lag[:LAG_ROWS])
         )
-        scale = masks[chunk] / jnp.maximum(summed[LAGS : LAGS + 1], 1.0)
+        scale = masks[chunk] / jnp.maximum(summed[:, LAGS : LAGS + 1], 1.0)
         result = (summed * scale).astype(jnp.bfloat16)
         for i in range(4):
-            out_ref[i, :, 4 * COLS * chunk : 4 * COLS * (chunk + 1)] = result[
-                :LAGS, 4 * COLS * i : 4 * COLS * (i + 1)
+            out_ref[i, 4 * COLS * chunk : 4 * COLS * (chunk + 1), :] = result[
+                4 * COLS * i : 4 * COLS * (i + 1), :LAGS
             ]
 
     def sent(k, carry):
@@ -336,14 +354,18 @@
 def on_device(raw, fir, spatial_taps, flags, keep):
     n = lax.axis_size("chan")
     vmem = pl.BlockSpec(memory_space=pltpu.VMEM)
-    smem = pl.BlockSpec(memory_space=pltpu.SMEM)
-    anywhere = pl.BlockSpec(memory_space=pl.ANY)
-    return pl.pallas_call(
+    hbm = pl.BlockSpec(memory_space=pltpu.HBM)
+    out = pl.pallas_call(
         functools.partial(kernel, n),
-        out_shape=jax.ShapeDtypeStruct((4, LAGS, 4 * n), jnp.bfloat16),
-        in_specs=[vmem, vmem, smem, smem, vmem, anywhere, anywhere],
+        out_shape=jax.ShapeDtypeStruct((4, 4 * n, LAGS), jnp.bfloat16),
+        in_specs=[hbm] * 7,
         out_specs=vmem,
         scratch_shapes=[
+            pltpu.VMEM(raw.shape, jnp.float32),
+            pltpu.VMEM((1, TAPS), jnp.float32),
+            pltpu.SMEM((SPAN,), jnp.float32),
+            pltpu.SMEM((S, 4), jnp.int32),
+            pltpu.VMEM((1, 4 * n), jnp.int32),
             pltpu.VMEM((NT, 4 * NF), jnp.bfloat16),
             pltpu.VMEM((2 * LAG_ROWS, 2 * NF), jnp.bfloat16),
             pltpu.VMEM((32, 384), jnp.float32),
@@ -357,24 +379,25 @@
             pltpu.VMEM((n, ROWS, NF), jnp.bfloat16),
             pltpu.VMEM((16 * COLS, 2 * NF), jnp.bfloat16),
             pltpu.VMEM((16 * COLS, 2 * NF), jnp.bfloat16),
-            pltpu.SemaphoreType.DMA((2,)),
+            pltpu.SemaphoreType.DMA((7,)),
             pltpu.SemaphoreType.DMA((2,)),
             pltpu.SemaphoreType.DMA((2,)),
             pltpu.SemaphoreType.DMA((n,)),
             pltpu.SemaphoreType.DMA((n,)),
         ],
         compiler_params=pltpu.CompilerParams(
-            collective_id=0, has_side_effects=True, vmem_limit_bytes=32 * 2**20
+            collective_id=0, has_side_effects=True, vmem_limit_bytes=65400 * 1024
         ),
     )(
         raw,
         fir.reshape(1, TAPS),
         spatial_taps,
-        flags,
+        flags.T,
         keep.reshape(1, 4 * n),
         jnp.asarray(dft_table()),
         jnp.asarray(lag_table()),
     )
+    return jnp.swapaxes(out, 1, 2)
 
 
 def solution(mesh):

time: 21.9 us -> 17.9 us (0.82)
  local copies, waits for them, and re-layouts: 5.17 us -> 1.47 us
    unnamed x15 -> x1, local copies, waits for them, and re-layouts: 4.43 us -> 1.47 us
    pallas_call x1 -> x0, local copies, waits for them, and re-layouts: 0.73 us -> none  [on_device(): pl.pallas_call(functools.partial(kernel, n), out_shape=jax.ShapeDtypeStru...]
where the time goes in v2:
time: 17.9 us; the launch traced here: 17.8 us
  Pallas kernels  16.3 us (91%)
  local copies, waits for them, and re-layouts  1.47 us (8%)
    pallas_call x1, Pallas kernels, on_device(): pl.pallas_call(functools.partial(kernel, n), out_shape=jax.ShapeDtypeStru...  16.3 us
    unnamed x1, local copies, waits for them, and re-layouts  1.47 us

profile of v2, /device:TPU:0, one launch (start us, length us, event | category | flops | bytes accessed | tf_op | source)
XLA Modules:
  0.0 17.8 jit_solution(13191236500289905675)
XLA Ops:
  0.0 16.3 %shard_map.73 = bf16[4,64,101]{2,1,0:T(8,128)(2,1)} custom-call(f32[4,2,4352]{2,1,0:T(2,128)} %raw_hbm.1, f32[1,255]{1,0:T(1,128)} %bitcast.5, f32[9]{0:T(128)} %taps_hbm.1, s32[2,4]{1,0:T(2,128)} %bitcast.6, s32[1,64]{1,0:T(1,128)} %bitcast.7, bf16[512,1024]{1,0:T(8,128)(2,1)} %constant.4.clone.dft_hbm, bf16[256,512]{1,0:T(8,128)(2,1)} %constant.5.clone.lag_hbm), custom_call_target="tpu_custom_call" | custom-call | tf_op jit(solution)/shard_map/pallas_call | solution.py:358
  16.3 1.5 %copy.9 = bf16[4,101,64]{1,2,0:T(8,128)(2,1)} copy(bf16[4,101,64]{1,2,0:T(8,128)(2,1)} %bitcast.4) | data formatting | bytes 103424

commit v3 on v2

--- a/solution.py
+++ b/solution.py
@@ -99,6 +99,7 @@
     halo_send,
     halo_recv,
     send_sem,
+    pass_sem,
     recv_sem,
 ):
     me = lax.axis_index("chan")
@@ -123,11 +124,16 @@
     barrier = pltpu.get_barrier_semaphore()
 
     def greet(k, carry):
-        peer = lax.rem(me + k, n)
+        peer = lax.rem(me + 2 * k, n)
         pl.semaphore_signal(barrier, inc=1, device_id={"chan": peer}, device_id_type=MESH)
         return carry
 
-    lax.fori_loop(1, n, greet, 0)
+    core = lax.rem(me, 2)
+    partner = me + 1 - 2 * core
+    across = lax.rem(me + n - 1 + 2 * core, n)
+    for peer in (partner, across):
+        pl.semaphore_signal(barrier, inc=1, device_id={"chan": peer}, device_id_type=MESH)
+    lax.fori_loop(1, n // 2, greet, 0)
 
     firs_ref[...] = jnp.zeros_like(firs_ref)
     fir_copy.wait()
@@ -163,7 +169,7 @@
     for b in range(TD // BLOCK):
         pad_ref[8:16, BLOCK * b : BLOCK * (b + 1)] = sums[8 * b : 8 * b + 8]
 
-    pl.semaphore_wait(barrier, n - 1)
+    pl.semaphore_wait(barrier, n // 2 + 1)
 
     to_right = pltpu.make_async_remote_copy(
         src_ref=pad_ref.at[8:16],
@@ -255,21 +261,25 @@
     spec = jnp.where(is_real, real, imag)
     all_ref[me] = jnp.where(stash, flag, spec).astype(jnp.bfloat16)
 
-    def copy_to(k):
+    def copy_block(src, peer, sem):
         return pltpu.make_async_remote_copy(
-            src_ref=all_ref.at[me],
-            dst_ref=all_ref.at[me],
-            send_sem=send_sem.at[k],
-            recv_sem=recv_sem.at[me],
-            device_id={"chan": lax.rem(me + k, n)},
+            src_ref=all_ref.at[src],
+            dst_ref=all_ref.at[src],
+            send_sem=sem,
+            recv_sem=recv_sem.at[src],
+            device_id={"chan": peer},
             device_id_type=MESH,
         )
 
+    def own_copy(k):
+        return copy_block(me, lax.rem(me + n - 2 * k, n), send_sem.at[k])
+
     def send(k, carry):
-        copy_to(k).start()
+        own_copy(k).start()
         return carry
 
-    lax.fori_loop(1, n, send, 0)
+    copy_block(me, partner, send_sem.at[0]).start()
+    lax.fori_loop(1, n // 2, send, 0)
 
     spec_ref[...] = jnp.where(stash, 0.0, spec)
     turn_ref[...] = jnp.where(stash, flag, jnp.where(is_real, imag, -real))
@@ -282,24 +292,34 @@
                 target[i, 8 * k : 8 * k + 8] = jnp.where(upper, first, second)
     lag_copy.wait()
 
-    def receive(k, carry):
-        src = lax.rem(me + k, n)
-        pltpu.make_async_remote_copy(
-            src_ref=all_ref.at[src],
-            dst_ref=all_ref.at[src],
-            send_sem=send_sem.at[k],
-            recv_sem=recv_sem.at[src],
-            device_id={"chan": src},
-            device_id_type=MESH,
-        ).wait_recv()
-        return carry
-
-    lax.fori_loop(1, n, receive, 0)
-
+    def pass_on(plane):
+        for chip in range(2):
+            src = 4 * plane + 2 * chip + core
+
+            @pl.when(src != me)
+            def _():
+                copy_block(src, partner, pass_sem.at[src]).wait_recv()
+                copy_block(src, partner, pass_sem.at[src]).start()
+
+    quads = COLS // 4
     for chunk in range(n // COLS):
 
+        def local_of(q):
+            return lax.rem(me // 4 + q, quads)
+
+        pass_on(chunk * quads + local_of(0))
+
         def quad(q, carry):
-            base = chunk * COLS + 4 * q
+            local = local_of(q)
+
+            @pl.when(q < quads - 1)
+            def _():
+                pass_on(chunk * quads + local_of(q + 1))
+
+            base = chunk * COLS + 4 * local
+            for chip in range(2):
+                src = base + 2 * chip + 1 - core
+                copy_block(src, partner, pass_sem.at[src]).wait_recv()
             for i in range(4):
                 for half, ref in enumerate((own_ref, own_turn_ref)):
                     sums = []
@@ -316,12 +336,12 @@
                             jnp.where(upper, a, b) + pltpu.roll(jnp.where(upper, b, a), 4, 0)
                         )
                     high, low = split(jnp.concatenate(both, 0))
-                    at = pl.ds(pl.multiple_of(4 * COLS * i + 16 * q, 16), 16)
+                    at = pl.ds(pl.multiple_of(4 * COLS * i + 16 * local, 16), 16)
                     cross_hi_ref[at, NF * half : NF * (half + 1)] = high
                     cross_lo_ref[at, NF * half : NF * (half + 1)] = low
             return carry
 
-        lax.fori_loop(0, COLS // 4, quad, 0)
+        lax.fori_loop(0, quads, quad, 0)
         lag = lag_ref[...]
         summed = product_nt(cross_hi_ref[...], lag)
         summed = (
@@ -336,11 +356,15 @@
                 4 * COLS * i : 4 * COLS * (i + 1), :LAGS
             ]
 
+    copy_block(me, partner, send_sem.at[0]).wait_send()
+
     def sent(k, carry):
-        copy_to(k).wait_send()
+        own_copy(k).wait_send()
+        src = lax.rem(me + 2 * k, n)
+        copy_block(src, partner, pass_sem.at[src]).wait_send()
         return carry
 
-    lax.fori_loop(1, n, sent, 0)
+    lax.fori_loop(1, n // 2, sent, 0)
 
     @pl.when(me < n - 1)
     def _():
@@ -357,7 +381,7 @@
     hbm = pl.BlockSpec(memory_space=pltpu.HBM)
     out = pl.pallas_call(
         functools.partial(kernel, n),
-        out_shape=jax.ShapeDtypeStruct((4, 4 * n, LAGS), jnp.bfloat16),
+        out_shape=pltpu.VMEM((4, 4 * n, LAGS), jnp.bfloat16),
         in_specs=[hbm] * 7,
         out_specs=vmem,
         scratch_shapes=[
@@ -382,20 +406,26 @@
             pltpu.SemaphoreType.DMA((7,)),
             pltpu.SemaphoreType.DMA((2,)),
             pltpu.SemaphoreType.DMA((2,)),
+            pltpu.SemaphoreType.DMA((n // 2,)),
             pltpu.SemaphoreType.DMA((n,)),
             pltpu.SemaphoreType.DMA((n,)),
         ],
         compiler_params=pltpu.CompilerParams(
-            collective_id=0, has_side_effects=True, vmem_limit_bytes=65400 * 1024
+            collective_id=0, has_side_effects=True, vmem_limit_bytes=48 * 2**20
         ),
     )(
-        raw,
-        fir.reshape(1, TAPS),
-        spatial_taps,
-        flags.T,
-        keep.reshape(1, 4 * n),
-        jnp.asarray(dft_table()),
-        jnp.asarray(lag_table()),
+        *[
+            pltpu.with_memory_space_constraint(value, pltpu.HBM)
+            for value in (
+                raw,
+                fir.reshape(1, TAPS),
+                spatial_taps,
+                flags.T,
+                keep.reshape(1, 4 * n),
+                jnp.asarray(dft_table()),
+                jnp.asarray(lag_table()),
+            )
+        ]
     )
     return jnp.swapaxes(out, 1, 2)
 

time: 17.9 us -> 15.9 us (0.89)
  Pallas kernels: 16.3 us -> 15.2 us
  local copies, waits for them, and re-layouts: 1.47 us -> 0.63 us
    pallas_call x1, Pallas kernels: 16.3 us -> 15.2 us  [on_device(): pl.pallas_call(functools.partial(kernel, n), out_shape=pltpu.VMEM((4, 4 *...]
    unnamed x1, local copies, waits for them, and re-layouts: 1.47 us -> 0.63 us
where the time goes in v3:
time: 15.9 us; the launch traced here: 15.8 us
  Pallas kernels  15.2 us (96%)
  local copies, waits for them, and re-layouts  0.63 us (4%)
    pallas_call x1, Pallas kernels, on_device(): pl.pallas_call(functools.partial(kernel, n), out_shape=pltpu.VMEM((4, 4 *...  15.2 us
    unnamed x1, local copies, waits for them, and re-layouts  0.63 us

profile of v3, /device:TPU:0, one launch (start us, length us, event | category | flops | bytes accessed | tf_op | source)
XLA Modules:
  0.0 15.8 jit_solution(16521353913474319989)
XLA Ops:
  0.0 15.2 %shard_map.73 = bf16[4,64,101]{2,1,0:T(8,128)(2,1)S(1)} custom-call(f32[4,2,4352]{2,1,0:T(2,128)} %raw_hbm.1, f32[1,255]{1,0:T(1,128)} %bitcast.5, f32[9]{0:T(128)} %taps_hbm.1, s32[2,4]{1,0:T(2,128)} %bitcast.6, s32[1,64]{1,0:T(1,128)} %bitcast.7, bf16[512,1024]{1,0:T(8,128)(2,1)} %constant.4.clone.dft_hbm, bf16[256,512]{1,0:T(8,128)(2,1)} %constant.5.clone.lag_hbm), custom_call_target="tpu_custom_call" | custom-call | tf_op jit(solution)/shard_map/pallas_call | solution.py:382
  15.2 0.6 %copy.9 = bf16[4,101,64]{1,2,0:T(8,128)(2,1)} copy(bf16[4,101,64]{1,2,0:T(8,128)(2,1)S(1)} %bitcast.4) | data formatting | bytes 103424

commit v4 on v3

--- a/solution.py
+++ b/solution.py
@@ -166,22 +166,39 @@
     sums = sums[:count, :BLOCK] + (
         sums[count:, :BLOCK] + sums[:count, BLOCK:] + sums[count:, BLOCK:]
     )
-    for b in range(TD // BLOCK):
-        pad_ref[8:16, BLOCK * b : BLOCK * (b + 1)] = sums[8 * b : 8 * b + 8]
+    per = NT // BLOCK
+    windows = jnp.concatenate(
+        [
+            jnp.concatenate([sums[8 * b : 8 * b + 8] for b in range(per * w, per * (w + 1))], 1)
+            for w in range(W)
+        ],
+        0,
+    )
+    win_hi, win_lo = split(windows)
+    dft_copy.wait()
+    spectra = jnp.dot(
+        jnp.concatenate([win_hi, win_lo], 0), dft_ref[...], preferred_element_type=jnp.float32
+    )
+    half = 8 * W
+    spectra = spectra[:half, : 2 * NF] + (
+        spectra[half:, : 2 * NF] + spectra[:half, 2 * NF :] + spectra[half:, 2 * NF :]
+    )
+    for w in range(W):
+        pad_ref[w, 8:16] = spectra[8 * w : 8 * w + 8]
 
     pl.semaphore_wait(barrier, n // 2 + 1)
 
     to_right = pltpu.make_async_remote_copy(
-        src_ref=pad_ref.at[8:16],
-        dst_ref=pad_ref.at[0:8],
+        src_ref=pad_ref.at[:, 8:16],
+        dst_ref=pad_ref.at[:, 0:8],
         send_sem=halo_send.at[0],
         recv_sem=halo_recv.at[0],
         device_id={"chan": lax.rem(me + 1, n)},
         device_id_type=MESH,
     )
     to_left = pltpu.make_async_remote_copy(
-        src_ref=pad_ref.at[8:16],
-        dst_ref=pad_ref.at[16:24],
+        src_ref=pad_ref.at[:, 8:16],
+        dst_ref=pad_ref.at[:, 16:24],
         send_sem=halo_send.at[1],
         recv_sem=halo_recv.at[1],
         device_id={"chan": lax.rem(me + n - 1, n)},
@@ -207,45 +224,6 @@
         masks.append(jnp.sum(hit, axis=1, keepdims=True))
     taps_copy.wait()
     flags_copy.wait()
-
-    @pl.when(me > 0)
-    def _():
-        to_right.wait_recv()
-
-    @pl.when(me == 0)
-    def _():
-        pad_ref[0:8] = jnp.zeros((8, TD), jnp.float32)
-
-    @pl.when(me < n - 1)
-    def _():
-        to_left.wait_recv()
-
-    @pl.when(me == n - 1)
-    def _():
-        pad_ref[16:24] = jnp.zeros((8, TD), jnp.float32)
-
-    filtered = taps_ref[0] * pad_ref[0:8]
-    for offset in range(1, SPAN):
-        filtered = filtered + taps_ref[offset] * pad_ref[2 * offset : 2 * offset + 8]
-    for tile in range(TD // 128):
-        filt_ref[8 * tile : 8 * tile + 8] = filtered[:, 128 * tile : 128 * (tile + 1)]
-    for s in range(S):
-        for tile in range(TD // 128):
-            one = filt_ref[pl.ds(8 * tile + s, 4, stride=2), :]
-            dup_ref[8 * s : 8 * s + 4, 128 * tile : 128 * (tile + 1)] = one
-            dup_ref[8 * s + 4 : 8 * s + 8, 128 * tile : 128 * (tile + 1)] = one
-    windows = jnp.concatenate(
-        [dup_ref[8 * s : 8 * s + 8, NT * w : NT * (w + 1)] for s in range(S) for w in range(W)], 0
-    )
-    win_hi, win_lo = split(windows)
-    dft_copy.wait()
-    spectra = jnp.dot(
-        jnp.concatenate([win_hi, win_lo], 0), dft_ref[...], preferred_element_type=jnp.float32
-    )
-    spectra = spectra[:ROWS, : 2 * NF] + (
-        spectra[ROWS:, : 2 * NF] + spectra[:ROWS, 2 * NF :] + spectra[ROWS:, 2 * NF :]
-    )
-    real, imag = spectra[:, :NF], spectra[:, NF:]
     rows = lax.broadcasted_iota(jnp.int32, (ROWS, NF), 0)
     lanes = lax.broadcasted_iota(jnp.int32, (ROWS, NF), 1)
     flag = jnp.zeros((ROWS, NF), jnp.float32)
@@ -253,6 +231,38 @@
         for c in range(4):
             here = (rows // 16 == s) & (rows % 4 == c)
             flag = jnp.where(here, flags_ref[s, c].astype(jnp.float32), flag)
+
+    @pl.when(me > 0)
+    def _():
+        to_right.wait_recv()
+
+    @pl.when(me == 0)
+    def _():
+        pad_ref[:, 0:8] = jnp.zeros((W, 8, 2 * NF), jnp.float32)
+
+    @pl.when(me < n - 1)
+    def _():
+        to_left.wait_recv()
+
+    @pl.when(me == n - 1)
+    def _():
+        pad_ref[:, 16:24] = jnp.zeros((W, 8, 2 * NF), jnp.float32)
+
+    for w in range(W):
+        filtered = taps_ref[0] * pad_ref[w, 0:8]
+        for offset in range(1, SPAN):
+            filtered = filtered + taps_ref[offset] * pad_ref[w, 2 * offset : 2 * offset + 8]
+        tiles = 2 * NF // 128
+        for tile in range(tiles):
+            at = 8 * (tiles * w + tile)
+            filt_ref[at : at + 8] = filtered[:, 128 * tile : 128 * (tile + 1)]
+            for s in range(S):
+                one = filt_ref[pl.ds(at + s, 4, stride=2), :]
+                row = 8 * (W * s + w)
+                dup_ref[row : row + 4, 128 * tile : 128 * (tile + 1)] = one
+                dup_ref[row + 4 : row + 8, 128 * tile : 128 * (tile + 1)] = one
+    spectra = dup_ref[...]
+    real, imag = spectra[:, :NF], spectra[:, NF:]
     factor = flag / jnp.maximum(jnp.sqrt(real * real + imag * imag), 0.25)
     is_real = (rows // 4) % 2 == 0
     real = (real * factor).astype(jnp.bfloat16).astype(jnp.float32)
@@ -272,7 +282,7 @@
         )
 
     def own_copy(k):
-        return copy_block(me, lax.rem(me + n - 2 * k, n), send_sem.at[k])
+        return copy_block(me, lax.rem(me + 2 * k, n), send_sem.at[k])
 
     def send(k, carry):
         own_copy(k).start()
@@ -305,7 +315,7 @@
     for chunk in range(n // COLS):
 
         def local_of(q):
-            return lax.rem(me // 4 + q, quads)
+            return lax.rem(me // 4 + quads - q, quads)
 
         pass_on(chunk * quads + local_of(0))
 
@@ -393,9 +403,9 @@
             pltpu.VMEM((NT, 4 * NF), jnp.bfloat16),
             pltpu.VMEM((2 * LAG_ROWS, 2 * NF), jnp.bfloat16),
             pltpu.VMEM((32, 384), jnp.float32),
-            pltpu.VMEM((24, TD), jnp.float32),
+            pltpu.VMEM((W, 24, 2 * NF), jnp.float32),
             pltpu.VMEM((TD // 16, 128), jnp.float32),
-            pltpu.VMEM((16, TD), jnp.float32),
+            pltpu.VMEM((ROWS, 2 * NF), jnp.float32),
             pltpu.VMEM((ROWS, NF), jnp.float32),
             pltpu.VMEM((ROWS, NF), jnp.float32),
             pltpu.VMEM((4, ROWS, NF), jnp.float32),

time: 15.9 us -> 15.2 us (0.956)
  Pallas kernels: 15.2 us -> 14.4 us
    pallas_call x1, Pallas kernels: 15.2 us -> 14.4 us  [on_device(): pl.pallas_call(functools.partial(kernel, n), out_shape=pltpu.VMEM((4, 4 *...]
where the time goes in v4:
time: 15.2 us; the launch traced here: 15.1 us
  Pallas kernels  14.4 us (95%)
  local copies, waits for them, and re-layouts  0.63 us (4%)
    pallas_call x1, Pallas kernels, on_device(): pl.pallas_call(functools.partial(kernel, n), out_shape=pltpu.VMEM((4, 4 *...  14.4 us
    unnamed x1, local copies, waits for them, and re-layouts  0.63 us

profile of v4, /device:TPU:0, one launch (start us, length us, event | category | flops | bytes accessed | tf_op | source)
XLA Modules:
  0.0 15.1 jit_solution(4969680487268130878)
XLA Ops:
  0.0 14.4 %shard_map.73 = bf16[4,64,101]{2,1,0:T(8,128)(2,1)S(1)} custom-call(f32[4,2,4352]{2,1,0:T(2,128)} %raw_hbm.1, f32[1,255]{1,0:T(1,128)} %bitcast.5, f32[9]{0:T(128)} %taps_hbm.1, s32[2,4]{1,0:T(2,128)} %bitcast.6, s32[1,64]{1,0:T(1,128)} %bitcast.7, bf16[512,1024]{1,0:T(8,128)(2,1)} %constant.4.clone.dft_hbm, bf16[256,512]{1,0:T(8,128)(2,1)} %constant.5.clone.lag_hbm), custom_call_target="tpu_custom_call" | custom-call | tf_op jit(solution)/shard_map/pallas_call | solution.py:392
  14.4 0.6 %copy.9 = bf16[4,101,64]{1,2,0:T(8,128)(2,1)} copy(bf16[4,101,64]{1,2,0:T(8,128)(2,1)S(1)} %bitcast.4) | data formatting | bytes 103424

commit v5 on v4

--- a/solution.py
+++ b/solution.py
@@ -133,7 +133,7 @@
     across = lax.rem(me + n - 1 + 2 * core, n)
     for peer in (partner, across):
         pl.semaphore_signal(barrier, inc=1, device_id={"chan": peer}, device_id_type=MESH)
-    lax.fori_loop(1, n // 2, greet, 0)
+    lax.fori_loop(1, n // 2, greet, 0, unroll=True)
 
     firs_ref[...] = jnp.zeros_like(firs_ref)
     fir_copy.wait()
@@ -289,7 +289,7 @@
         return carry
 
     copy_block(me, partner, send_sem.at[0]).start()
-    lax.fori_loop(1, n // 2, send, 0)
+    lax.fori_loop(1, n // 2, send, 0, unroll=True)
 
     spec_ref[...] = jnp.where(stash, 0.0, spec)
     turn_ref[...] = jnp.where(stash, flag, jnp.where(is_real, imag, -real))
@@ -374,7 +374,7 @@
         copy_block(src, partner, pass_sem.at[src]).wait_send()
         return carry
 
-    lax.fori_loop(1, n // 2, sent, 0)
+    lax.fori_loop(1, n // 2, sent, 0, unroll=True)
 
     @pl.when(me < n - 1)
     def _():

time: 15.2 us -> 15.2 us (level)
  no operation moved by 1% of the time
where the time goes in v5:
time: 15.2 us; the launch traced here: 15 us
  Pallas kernels  14.4 us (95%)
  local copies, waits for them, and re-layouts  0.63 us (4%)
    pallas_call x1, Pallas kernels, on_device(): pl.pallas_call(functools.partial(kernel, n), out_shape=pltpu.VMEM((4, 4 *...  14.4 us
    unnamed x1, local copies, waits for them, and re-layouts  0.63 us

profile of v5, /device:TPU:0, one launch (start us, length us, event | category | flops | bytes accessed | tf_op | source)
XLA Modules:
  0.0 15.0 jit_solution(6301004725143105792)
XLA Ops:
  0.0 14.4 %shard_map.73 = bf16[4,64,101]{2,1,0:T(8,128)(2,1)S(1)} custom-call(f32[4,2,4352]{2,1,0:T(2,128)} %raw_hbm.1, f32[1,255]{1,0:T(1,128)} %bitcast.5, f32[9]{0:T(128)} %taps_hbm.1, s32[2,4]{1,0:T(2,128)} %bitcast.6, s32[1,64]{1,0:T(1,128)} %bitcast.7, bf16[512,1024]{1,0:T(8,128)(2,1)} %constant.4.clone.dft_hbm, bf16[256,512]{1,0:T(8,128)(2,1)} %constant.5.clone.lag_hbm), custom_call_target="tpu_custom_call" | custom-call | tf_op jit(solution)/shard_map/pallas_call | solution.py:392
  14.4 0.6 %copy.9 = bf16[4,101,64]{1,2,0:T(8,128)(2,1)} copy(bf16[4,101,64]{1,2,0:T(8,128)(2,1)S(1)} %bitcast.4) | data formatting | bytes 103424
